TPU v7x, 256 devices: a whole 4x4x8 slice. The times are simulated.
256 devices in a mesh: sample: 4 (over y_lo, core), row: 16 (over z, y_hi), col: 4 (over x).
Axes of the slice: x: 4, y: 4 (y_hi: 2, y_lo: 2; y = y_hi * 2 + y_lo), z: 8, core: 2. Of those that a mesh axis runs over, the one named last changes fastest.
Arguments:
- trunk_pair: bfloat16 [1024, 1024, 128], P('row', 'col'), may hold values from -6 to 6
- distance_bins: int32 [4, 1024, 1024], P('sample', 'row', 'col'), may hold values from 0 to 38
- token_mask: int32 [1024], replicated, may hold values 0 or 1
- single: bfloat16 [1024, 384], P('row', 'sample'), may hold values from -6 to 6
- dist_weight: bfloat16 [39, 128], replicated, may hold values from -5 to 5
- pair_gain: float32 [128], replicated, may hold values from 0.1 to 1.9
- bias_weight: bfloat16 [128, 16], replicated
- single_gain: float32 [384], replicated, may hold values from 0.1 to 1.9
- query_weight: bfloat16 [384, 384], P(None, 'col'), may hold values from -0.3125 to 0.3125
- query_bias: float32 [384], P('col'), may hold values from -3 to 3
- key_weight: bfloat16 [384, 384], P(None, 'col'), may hold values from -0.3125 to 0.3125
- value_weight: bfloat16 [384, 384], P(None, 'col'), may hold values from -0.3125 to 0.3125
- gate_weight: bfloat16 [384, 384], P(None, 'col'), may hold values from -0.3125 to 0.3125
- out_weight: bfloat16 [384, 384], P('col'), may hold values from -0.3125 to 0.3125
Outputs:
- single_update: bfloat16 [4, 1024, 384], P('sample', 'row', 'col')
All inputs are finite; a program needn't handle non-finite values.
Results may differ from a plain program's by a relative error of at most 0.015.
The roundings to bfloat16 on the way count: a program that leaves them out, or rounds other values in their place, can miss the bound.
Values may be sent and summed in bfloat16 or wider, within the bound.
No kernel may reach another device: no remote copies, remote signals or barrier semaphores. Data moves between devices by JAX's collectives and lax.ppermute only.
A program may use at most 64 MiB of HBM per device.

v0:
```python
import jax
import jax.numpy as jnp
from jax import lax
from jax.sharding import PartitionSpec as P


def layer_norm(values, gain):
    mean = jnp.mean(values, axis=-1, keepdims=True)
    centered = values - mean
    var = jnp.mean(centered * centered, axis=-1, keepdims=True)
    return centered * lax.rsqrt(var + 1e-05) * gain


def attend_block(carry, q_heads, key_block, value_block, bias_part, mask_part):
    running_max, running_sum, running_acc = carry
    scale = 1.0 / jnp.sqrt(jnp.float32(q_heads.shape[2]))
    scores = (
        jnp.einsum("hqd,khd->hqk", q_heads, key_block, preferred_element_type=jnp.float32) * scale
    )
    scores = scores + bias_part.astype(jnp.float32)
    scores = scores + ((mask_part.astype(jnp.float32) - 1.0) * 1000000000.0)[None, None, :]
    new_max = jnp.maximum(running_max, jnp.max(scores, axis=-1))
    weights = jnp.exp(scores - new_max[..., None])
    new_sum = jnp.sum(weights, axis=-1)
    contrib = jnp.einsum(
        "hqk,khd->hqd",
        weights.astype(jnp.bfloat16),
        value_block,
        preferred_element_type=jnp.float32,
    )
    return (new_max, new_sum, contrib)


def body(
    trunk_pair,
    distance_bins,
    token_mask,
    single,
    dist_weight,
    pair_gain,
    bias_weight,
    single_gain,
    query_weight,
    query_bias,
    key_weight,
    value_weight,
    gate_weight,
    out_weight,
):
    heads_total = bias_weight.shape[1]
    channels = trunk_pair.shape[2]
    group_width = query_weight.shape[1]
    head_dim = single_gain.shape[0] // heads_total
    group_heads = group_width // head_dim
    tile_rows = trunk_pair.shape[0]
    tile_cols = trunk_pair.shape[1]
    whole_single = lax.all_gather(single, "sample", axis=1, tiled=True)
    single_normed = layer_norm(whole_single.astype(jnp.float32), single_gain).astype(jnp.bfloat16)
    queries = (
        jnp.dot(single_normed, query_weight, preferred_element_type=jnp.float32) + query_bias
    ).astype(jnp.bfloat16)
    gate = jax.nn.sigmoid(jnp.dot(single_normed, gate_weight, preferred_element_type=jnp.float32))
    key_value_weight = jnp.concatenate([key_weight, value_weight], axis=1)
    padded_table = jnp.concatenate(
        [dist_weight, jnp.zeros((128 - dist_weight.shape[0], channels), jnp.bfloat16)], axis=0
    )
    onehot = (distance_bins[0][..., None] == jnp.arange(128, dtype=jnp.int32)).astype(jnp.bfloat16)
    embedded = jnp.dot(onehot.reshape(-1, 128), padded_table, preferred_element_type=jnp.float32)
    pair_s = trunk_pair.reshape(-1, channels).astype(jnp.float32) + embedded
    pair_normed = layer_norm(pair_s, pair_gain).astype(jnp.bfloat16)
    bias_tile = lax.dot_general(
        bias_weight, pair_normed, (((0,), (1,)), ((), ())), preferred_element_type=jnp.float32
    )
    bias_tile = bias_tile.astype(jnp.bfloat16).reshape(heads_total, tile_rows, tile_cols)
    q_heads = jnp.transpose(queries.reshape(tile_rows, group_heads, head_dim), (1, 0, 2))
    bias_heads = lax.all_to_all(bias_tile, "col", split_axis=0, concat_axis=2, tiled=True)
    start_carry = (
        jnp.full((group_heads, tile_rows), -1e30, jnp.float32),
        jnp.zeros((group_heads, tile_rows), jnp.float32),
        jnp.zeros((group_heads, tile_rows, head_dim), jnp.float32),
    )
    piece = lax.all_gather(single_normed, "row", axis=0, tiled=True)
    count = piece.shape[0]
    projected = jnp.dot(piece, key_value_weight, preferred_element_type=jnp.float32).astype(
        jnp.bfloat16
    )
    key_block = projected[:, :group_width].reshape(count, group_heads, head_dim)
    value_block = projected[:, group_width:].reshape(count, group_heads, head_dim)
    final_max, final_sum, final_acc = attend_block(
        start_carry, q_heads, key_block, value_block, bias_heads, token_mask
    )
    attended = final_acc / final_sum[..., None]
    attended = jnp.transpose(attended, (1, 0, 2)).reshape(tile_rows, group_width)
    gated = (gate * attended).astype(jnp.bfloat16)
    partial_update = jnp.dot(gated, out_weight, preferred_element_type=jnp.float32)
    update = lax.psum_scatter(partial_update, "col", scatter_dimension=1, tiled=True)
    return update.astype(jnp.bfloat16)[None]


def solution(mesh):
    placed = (
        P("row", "col", None),
        P("sample", "row", "col"),
        P(),
        P("row", "sample"),
        P(),
        P(),
        P(),
        P(),
        P(None, "col"),
        P("col"),
        P(None, "col"),
        P(None, "col"),
        P(None, "col"),
        P("col", None),
    )
    return jax.shard_map(
        body, mesh=mesh, in_specs=placed, out_specs=P("sample", "row", "col"), check_vma=False
    )
```

profile of v0, /device:TPU:8, one launch (start us, length us, event | category | flops | bytes accessed | tf_op | source)
XLA Modules:
  0.0 121.4 jit_solution(10705247466023171844)
XLA Ops:
  6.5 0.0 copy-start
  6.5 5.1 %bitcast_convert_fusion = f32[16384,128]{1,0:T(8,128)} fusion(bf16[64,256,128]{2,1,0:T(8,128)(2,1)} %param.14), kind=kLoop, calls=%fused_computation.5 | loop fusion | flops 2097152 | bytes 12582912 | tf_op jit(solution)/shard_map/convert_element_type | solution.py:69
  11.7 9.1 %copy.31 = f32[16384,128]{0,1:T(8,128)} copy(f32[16384,128]{1,0:T(8,128)} %bitcast_convert_fusion) | data formatting | bytes 16777216 | tf_op jit(solution)/shard_map/convert_element_type | solution.py:69
  20.7 0.0 copy-done.5
  20.8 0.0 copy-done.7
  20.8 7.9 %fusion.26 = (f32[16384]{0:T(1024)S(1)}, f32[16384,128]{0,1:T(8,128)S(1)}) fusion(f32[16384,128]{0,1:T(8,128)} %copy.31, bf16[39,128]{1,0:T(8,128)(2,1)S(1)} %copy-done.7, s32[16384]{0:T(1024)S(1)} %bitcast.53), kind=kOutput, calls=%fused_computation.49 | convolution fusion | flops 543145984 | bytes 16918272 | tf_op jit(solution)/shard_map/dot_general | solution.py:68
  28.7 0.0 copy-start.8
  28.7 0.0 copy-start.11
  28.8 0.0 copy-start.6
  28.8 0.0 copy-start.10
  28.8 1.0 multiply_reduce_fusion
  29.8 0.0 copy-start.1
  29.8 0.0 copy-start.12
  29.8 0.0 copy-start.3
  29.8 0.0 copy-start.4
  29.8 0.0 copy-start.9
  29.8 0.0 copy-done.8
  29.8 0.0 copy-done.11
  29.9 1.1 convolution_convert_fusion
  31.0 0.9 copy.36
  31.9 4.3 %all-to-all-start = ((bf16[16,64,256]{2,1,0:T(8,128)(2,1)}), bf16[16,64,256]{2,1,0:T(8,128)(2,1)S(1)}, u32[]{:S(2)}, u32[]{:S(2)}) async-start(bf16[16,64,256]{2,1,0:T(8,128)(2,1)} %bitcast.27), calls=%async_computation | async-start | bytes 1048576 | tf_op jit(solution)/shard_map/all_to_all | solution.py:76
  36.2 0.0 reduce-scatter.4.cloned.1.call-start
  36.2 0.0 copy-done.6
  36.2 5.2 %all-gather = bf16[4,96,64]{1,2,0:T(8,128)(2,1)S(1)} all-gather(bf16[1,96,64]{1,2,0:T(8,128)(2,1)S(1)} %bitcast.58), channel_id=1, replica_groups=mesh['sample'=4,'row'=16,'col'=4] {'sample'}, dimensions={0}, use_global_device_ids=true | all-gather | bytes 61440 | tf_op jit(solution)/shard_map/all_gather | solution.py:57
  41.4 0.1 copy.26
  41.5 0.1 convert_reduce_fusion
  41.6 0.1 reshape.68
  41.8 0.2 multiply_reduce_fusion.1
  41.9 0.0 copy-done.10
  42.0 0.1 bitcast_convert_fusion.1
  42.0 47.7 %all_gather.7 = bf16[1024,384]{1,0:T(8,128)(2,1)S(1)} all-gather(bf16[64,384]{1,0:T(8,128)(2,1)S(1)} %bitcast_convert_fusion.1), channel_id=1, replica_groups=mesh['sample'=4,'row'=16,'col'=4] {'row'}, dimensions={0}, use_global_device_ids=true | all-gather | bytes 835584 | tf_op jit(solution)/shard_map/all_gather | solution.py:82
  89.8 0.2 fusion.12
  90.0 0.1 copy.27
  90.1 0.4 convolution_convert_fusion.1
  90.5 0.0 copy-done.9
  90.6 0.0 all-to-all-done
  90.6 0.1 convert_bitcast_fusion
  90.7 0.1 copy.34
  90.8 0.4 fusion.27
  91.3 0.3 fusion.13
  91.6 0.3 fusion.6
  92.0 0.1 copy.30
  92.0 0.0 copy-done
  92.1 0.0 copy-done.2
  92.1 1.0 convolution_bitcast_fusion
  93.1 0.0 reduce-scatter.4.cloned.1.call-update
  93.1 19.9 %reduce-scatter.4.cloned.1.call-done = f32[96,64]{1,0:T(8,128)} async-done(((f32[384,64]{1,0:T(8,128)}), f32[96,64]{1,0:T(8,128)}) %reduce-scatter.4.cloned.1.call-update) | async-done | bytes 24592
  113.0 1.5 %copy.33 = bf16[64,96]{1,0:T(8,128)(2,1)} copy(f32[64,96]{0,1:T(8,128)} %bitcast.57) | data formatting | bytes 36864
  (15 shorter events, 0.1 us)
Async XLA Ops:
  6.5 85.5 %copy-start = (bf16[96,384]{1,0:T(8,128)(2,1)S(1)}, bf16[96,384]{1,0:T(8,128)(2,1)}, u32[]{:S(2)}) copy-start(bf16[96,384]{1,0:T(8,128)(2,1)} %param.27) | copy-start | bytes 221188
  11.7 9.1 %copy-start.5 = (s32[1,64,256]{2,1,0:T(8,128)S(1)}, s32[1,64,256]{2,1,0:T(8,128)}, u32[]{:S(2)}) copy-start(s32[1,64,256]{2,1,0:T(8,128)} %param.15) | copy-start | bytes 196612
  11.7 9.1 %copy-start.7 = (bf16[39,128]{1,0:T(8,128)(2,1)S(1)}, bf16[39,128]{1,0:T(8,128)(2,1)}, u32[]{:S(2)}) copy-start(bf16[39,128]{1,0:T(8,128)(2,1)} %param.18) | copy-start | bytes 29956
  28.7 1.1 copy-start.8
  28.7 1.1 copy-start.11
  28.8 7.4 %copy-start.6 = (bf16[64,96]{1,0:T(8,128)(2,1)S(1)}, bf16[64,96]{1,0:T(8,128)(2,1)}, u32[]{:S(2)}) copy-start(bf16[64,96]{1,0:T(8,128)(2,1)} %param.17) | copy-start | bytes 36868
  28.8 13.2 %copy-start.10 = (f32[384]{0:T(512)S(1)}, f32[384]{0:T(512)}, u32[]{:S(2)}) copy-start(f32[384]{0:T(512)} %param.21) | copy-start | bytes 4612
  29.8 60.0 %copy-start.1 = (bf16[384,96]{0,1:T(8,128)(2,1)S(1)}, bf16[384,96]{0,1:T(8,128)(2,1)}, u32[]{:S(2)}) copy-start(bf16[384,96]{0,1:T(8,128)(2,1)} %param.22) | copy-start | bytes 221188
  29.8 60.0 %copy-start.12 = (f32[96]{0:T(128)S(1)}, f32[96]{0:T(128)}, u32[]{:S(2)}) copy-start(f32[96]{0:T(128)} %param.23) | copy-start | bytes 1156
  29.8 60.3 %copy-start.3 = (bf16[384,96]{0,1:T(8,128)(2,1)S(1)}, bf16[384,96]{0,1:T(8,128)(2,1)}, u32[]{:S(2)}) copy-start(bf16[384,96]{0,1:T(8,128)(2,1)} %param.25) | copy-start | bytes 221188
  29.8 60.3 %copy-start.4 = (bf16[384,96]{0,1:T(8,128)(2,1)S(1)}, bf16[384,96]{0,1:T(8,128)(2,1)}, u32[]{:S(2)}) copy-start(bf16[384,96]{0,1:T(8,128)(2,1)} %param.24) | copy-start | bytes 221188
  29.8 60.7 %copy-start.9 = (s32[1024]{0:T(1024)S(1)}, s32[1024]{0:T(1024)}, u32[]{:S(2)}) copy-start(s32[1024]{0:T(1024)} %param.16) | copy-start | bytes 12292
  31.0 61.1 %copy-start.2 = (bf16[384,96]{0,1:T(8,128)(2,1)S(1)}, bf16[384,96]{0,1:T(8,128)(2,1)}, u32[]{:S(2)}) copy-start(bf16[384,96]{0,1:T(8,128)(2,1)} %param.26) | copy-start | bytes 221188
  31.9 58.7 %all-to-all-start = ((bf16[16,64,256]{2,1,0:T(8,128)(2,1)}), bf16[16,64,256]{2,1,0:T(8,128)(2,1)S(1)}, u32[]{:S(2)}, u32[]{:S(2)}) async-start(bf16[16,64,256]{2,1,0:T(8,128)(2,1)} %bitcast.27), calls=%async_computation | async-start | bytes 1048576 | tf_op jit(solution)/shard_map/all_to_all | solution.py:76
  36.2 76.8 %reduce-scatter.4.cloned.1.call-start = ((), (), s32[]{:S(2)}) async-start(), calls=%async_computation.2 | async-start | bytes 245760
Sparse Core Ops, SparseCore 0:
  93.2 19.7 reduce-scatter.3
where the time goes:
time: 122 us; the launch traced here: 121 us
  blocking collectives  53 us (43%)
  waiting for transfers between devices  19.9 us (16%)
  between operations  13.7 us (11%)
  local copies, waits for them, and re-layouts  12.1 us (10%)
  matrix products  11.5 us (9%)
  other arithmetic  6.93 us (6%)
  starting transfers between devices  4.29 us (4%)
    all_gather x1, blocking collectives, body(): piece = lax.all_gather(single_normed, 'row', axis=0, tiled=True)  47.7 us
    unnamed x2, waiting for transfers between devices  19.9 us
    convert_element_type x1, local copies, waits for them, and re-layouts, body(): pair_s = trunk_pair.reshape(-1, channels).astype(jnp.float32) + embedded  9.08 us
    dot_general x1, matrix products, body(): jnp.dot(onehot.reshape(-1, 128), padded_table, preferred_element_type=jnp...  7.93 us
    all_gather x1, blocking collectives, body(): whole_single = lax.all_gather(single, 'sample', axis=1, tiled=True)  5.24 us
    convert_element_type x1, other arithmetic, body(): pair_s = trunk_pair.reshape(-1, channels).astype(jnp.float32) + embedded  5.11 us
    all_to_all x1, starting transfers between devices, body(): lax.all_to_all(bias_tile, 'col', split_axis=0, concat_axis=2, tiled=True)  4.29 us
    unnamed x29, local copies, waits for them, and re-layouts  2.51 us
  transfers between devices with their start and end apart: 2, of which 1 were waited for; matrix products, arithmetic and copies ran while one was open for 1% of the time, Pallas kernels for 0%

commit v1 on v0

--- a/solution.py
+++ b/solution.py
@@ -79,7 +79,9 @@
         jnp.zeros((group_heads, tile_rows), jnp.float32),
         jnp.zeros((group_heads, tile_rows, head_dim), jnp.float32),
     )
-    piece = lax.all_gather(single_normed, "row", axis=0, tiled=True)
+    piece = jnp.concatenate(
+        lax.all_to_all(jnp.stack([single_normed] * lax.axis_size("row")), "row", 0, 0), axis=0
+    )
     count = piece.shape[0]
     projected = jnp.dot(piece, key_value_weight, preferred_element_type=jnp.float32).astype(
         jnp.bfloat16

time: 122 us -> 109 us (0.89)
  blocking collectives: 53 us -> 5.23 us
  waiting for transfers between devices: 19.9 us -> 43.7 us
  starting transfers between devices: 4.29 us -> 14.6 us
    all_gather x1 -> x0, blocking collectives: 47.7 us -> none  [body(): piece = lax.all_gather(single_normed, 'row', axis=0, tiled=True)]
    all_to_all x0 -> x1, waiting for transfers between devices: none -> 22 us  [body(): lax.all_to_all(jnp.stack([single_normed] * lax.axis_size('row')), 'row',...]
    all_to_all x0 -> x1, starting transfers between devices: none -> 10.3 us  [body(): lax.all_to_all(jnp.stack([single_normed] * lax.axis_size('row')), 'row',...]
    all_to_all x1, waiting for transfers between devices: 0.01 us -> 3.64 us  [body(): lax.all_to_all(bias_tile, 'col', split_axis=0, concat_axis=2, tiled=True)]
    unnamed x2, waiting for transfers between devices: 19.9 us -> 18.1 us
  transfers between devices with their start and end apart: 2 -> 3, of which waited for: 1 -> 3; matrix products, arithmetic and copies ran while one was open for 1% -> 1% of each run, Pallas kernels for 0% -> 0%
where the time goes in v1:
time: 109 us
  waiting for transfers between devices  43.7 us (40%)
  starting transfers between devices  14.6 us (13%)
  between operations  13.7 us (13%)
  local copies, waits for them, and re-layouts  13.1 us (12%)
  matrix products  11.4 us (10%)
  other arithmetic  6.94 us (6%)
  blocking collectives  5.23 us (5%)
    all_to_all x1, waiting for transfers between devices, body(): lax.all_to_all(jnp.stack([single_normed] * lax.axis_size('row')), 'row',...  22 us
    unnamed x2, waiting for transfers between devices  18.1 us
    all_to_all x1, starting transfers between devices, body(): lax.all_to_all(jnp.stack([single_normed] * lax.axis_size('row')), 'row',...  10.3 us
    convert_element_type x1, local copies, waits for them, and re-layouts, body(): pair_s = trunk_pair.reshape(-1, channels).astype(jnp.float32) + embedded  9.02 us
    dot_general x1, matrix products, body(): jnp.dot(onehot.reshape(-1, 128), padded_table, preferred_element_type=jnp...  7.93 us
    all_gather x1, blocking collectives, body(): whole_single = lax.all_gather(single, 'sample', axis=1, tiled=True)  5.23 us
    convert_element_type x1, other arithmetic, body(): pair_s = trunk_pair.reshape(-1, channels).astype(jnp.float32) + embedded  5.12 us
    all_to_all x1, starting transfers between devices, body(): lax.all_to_all(bias_tile, 'col', split_axis=0, concat_axis=2, tiled=True)  4.29 us
  transfers between devices with their start and end apart: 3, of which 3 were waited for; matrix products, arithmetic and copies ran while one was open for 1% of the time, Pallas kernels for 0%

profile of v1, /device:TPU:8, one launch (start us, length us, event | category | flops | bytes accessed | tf_op | source)
XLA Modules:
  0.0 108.6 jit_solution(14331651830527900083)
XLA Ops:
  6.5 0.0 copy-start
  6.5 5.1 %bitcast_convert_fusion = f32[16384,128]{1,0:T(8,128)} fusion(bf16[64,256,128]{2,1,0:T(8,128)(2,1)} %param.14), kind=kLoop, calls=%fused_computation.5 | loop fusion | flops 2097152 | bytes 12582912 | tf_op jit(solution)/shard_map/convert_element_type | solution.py:69
  11.7 9.0 %copy.32 = f32[16384,128]{0,1:T(8,128)} copy(f32[16384,128]{1,0:T(8,128)} %bitcast_convert_fusion) | data formatting | bytes 16777216 | tf_op jit(solution)/shard_map/convert_element_type | solution.py:69
  20.7 0.0 copy-done.5
  20.7 0.0 copy-done.7
  20.7 7.9 %fusion.26 = (f32[16384]{0:T(1024)S(1)}, f32[16384,128]{0,1:T(8,128)S(1)}) fusion(f32[16384,128]{0,1:T(8,128)} %copy.32, bf16[39,128]{1,0:T(8,128)(2,1)S(1)} %copy-done.7, s32[16384]{0:T(1024)S(1)} %bitcast.55), kind=kOutput, calls=%fused_computation.49 | convolution fusion | flops 543145984 | bytes 16918272 | tf_op jit(solution)/shard_map/dot_general | solution.py:68
  28.7 0.0 copy-start.8
  28.7 0.0 copy-start.11
  28.7 0.0 copy-start.6
  28.7 0.0 copy-start.10
  28.7 1.0 multiply_reduce_fusion
  29.7 0.0 copy-start.1
  29.7 0.0 copy-start.12
  29.7 0.0 copy-start.9
  29.8 0.0 copy-done.8
  29.8 0.0 copy-done.11
  29.8 0.0 copy-start.3
  29.8 0.0 copy-start.4
  29.8 1.1 %convolution_convert_fusion = bf16[16384,16]{0,1:T(8,128)(2,1)S(1)} fusion(bf16[128,16]{0,1:T(8,128)(2,1)S(1)} %copy-done.8, f32[16384,128]{0,1:T(8,128)S(1)} %get-tuple-element.8, f32[128]{0:T(128)S(1)} %copy-done.11, f32[16384]{0:T(1024)S(1)} %add_rsqrt_fusion, f32[16384]{0:T(1024)S(1)} %broadcast_multiply_fusion), kind=kOutput, calls=%fused_computation.1 | convolution fusion | flops 75759616 | bytes 9048576 | tf_op jit(solution)/shard_map/dot_general | solution.py:71
  31.0 0.9 copy.37
  31.9 4.3 %all-to-all-start.1 = ((bf16[16,64,256]{2,1,0:T(8,128)(2,1)}), bf16[16,64,256]{2,1,0:T(8,128)(2,1)S(1)}, u32[]{:S(2)}, u32[]{:S(2)}) async-start(bf16[16,64,256]{2,1,0:T(8,128)(2,1)} %bitcast.28), calls=%async_computation.1 | async-start | bytes 1048576 | tf_op jit(solution)/shard_map/all_to_all | solution.py:76
  36.2 0.0 copy-done.6
  36.2 5.2 %all-gather = bf16[4,96,64]{1,2,0:T(8,128)(2,1)S(1)} all-gather(bf16[1,96,64]{1,2,0:T(8,128)(2,1)S(1)} %bitcast.60), channel_id=1, replica_groups=mesh['sample'=4,'row'=16,'col'=4] {'sample'}, dimensions={0}, use_global_device_ids=true | all-gather | bytes 61440 | tf_op jit(solution)/shard_map/all_gather | solution.py:57
  41.4 0.1 copy.27
  41.4 0.1 convert_reduce_fusion
  41.6 0.1 reshape.74
  41.7 0.2 multiply_reduce_fusion.1
  41.9 0.1 bitcast_convert_fusion.1
  42.0 3.6 %all-to-all-done.1 = bf16[16,64,256]{2,1,0:T(8,128)(2,1)S(1)} async-done(((bf16[16,64,256]{2,1,0:T(8,128)(2,1)}), bf16[16,64,256]{2,1,0:T(8,128)(2,1)S(1)}, u32[]{:S(2)}, u32[]{:S(2)}) %all-to-all-start.1) | async-done | bytes 524320 | tf_op jit(solution)/shard_map/all_to_all | solution.py:76
  45.6 1.0 stack.2
  46.6 10.3 %all-to-all-start = ((bf16[16,64,384]{2,1,0:T(8,128)(2,1)}), bf16[16,64,384]{2,1,0:T(8,128)(2,1)S(1)}, u32[]{:S(2)}, u32[]{:S(2)}) async-start(bf16[16,64,384]{2,1,0:T(8,128)(2,1)} %stack.2), calls=%async_computation | async-start | bytes 1572864 | tf_op jit(solution)/shard_map/all_to_all | solution.py:83
  56.9 0.0 reduce-scatter.4.cloned.1.call-start
  57.0 0.2 fusion.12
  57.2 0.1 copy.28
  57.3 0.0 copy-done.9
  57.3 0.1 convert_bitcast_fusion
  57.4 0.1 copy.35
  57.6 22.0 %all-to-all-done = bf16[16,64,384]{2,1,0:T(8,128)(2,1)S(1)} async-done(((bf16[16,64,384]{2,1,0:T(8,128)(2,1)}), bf16[16,64,384]{2,1,0:T(8,128)(2,1)S(1)}, u32[]{:S(2)}, u32[]{:S(2)}) %all-to-all-start) | async-done | bytes 786464 | tf_op jit(solution)/shard_map/all_to_all | solution.py:83
  79.5 0.4 convolution_convert_fusion.1
  80.0 0.4 fusion.27
  80.4 0.3 fusion.13
  80.8 0.3 fusion.6
  81.1 0.1 copy.31
  81.2 0.0 copy-done
  81.2 1.0 convolution_bitcast_fusion
  82.2 0.0 reduce-scatter.4.cloned.1.call-update
  82.3 18.0 %reduce-scatter.4.cloned.1.call-done = f32[96,64]{1,0:T(8,128)} async-done(((f32[384,64]{1,0:T(8,128)}), f32[96,64]{1,0:T(8,128)}) %reduce-scatter.4.cloned.1.call-update) | async-done | bytes 24592
  100.3 1.5 %copy.34 = bf16[64,96]{1,0:T(8,128)(2,1)} copy(f32[64,96]{0,1:T(8,128)} %bitcast.59) | data formatting | bytes 36864
  (17 shorter events, 0.1 us)
Async XLA Ops:
  6.5 74.7 %copy-start = (bf16[96,384]{1,0:T(8,128)(2,1)S(1)}, bf16[96,384]{1,0:T(8,128)(2,1)}, u32[]{:S(2)}) copy-start(bf16[96,384]{1,0:T(8,128)(2,1)} %param.27) | copy-start | bytes 221188
  11.7 9.0 %copy-start.5 = (s32[1,64,256]{2,1,0:T(8,128)S(1)}, s32[1,64,256]{2,1,0:T(8,128)}, u32[]{:S(2)}) copy-start(s32[1,64,256]{2,1,0:T(8,128)} %param.15) | copy-start | bytes 196612
  11.7 9.1 %copy-start.7 = (bf16[39,128]{1,0:T(8,128)(2,1)S(1)}, bf16[39,128]{1,0:T(8,128)(2,1)}, u32[]{:S(2)}) copy-start(bf16[39,128]{1,0:T(8,128)(2,1)} %param.18) | copy-start | bytes 29956
  28.7 1.1 %copy-start.8 = (bf16[128,16]{0,1:T(8,128)(2,1)S(1)}, bf16[128,16]{0,1:T(8,128)(2,1)}, u32[]{:S(2)}) copy-start(bf16[128,16]{0,1:T(8,128)(2,1)} %param.20) | copy-start | bytes 12292
  28.7 1.1 %copy-start.11 = (f32[128]{0:T(128)S(1)}, f32[128]{0:T(128)}, u32[]{:S(2)}) copy-start(f32[128]{0:T(128)} %param.19) | copy-start | bytes 1540
  28.7 7.4 %copy-start.6 = (bf16[64,96]{1,0:T(8,128)(2,1)S(1)}, bf16[64,96]{1,0:T(8,128)(2,1)}, u32[]{:S(2)}) copy-start(bf16[64,96]{1,0:T(8,128)(2,1)} %param.17) | copy-start | bytes 36868
  28.7 13.2 %copy-start.10 = (f32[384]{0:T(512)S(1)}, f32[384]{0:T(512)}, u32[]{:S(2)}) copy-start(f32[384]{0:T(512)} %param.21) | copy-start | bytes 4612
  29.7 27.3 %copy-start.1 = (bf16[384,96]{0,1:T(8,128)(2,1)S(1)}, bf16[384,96]{0,1:T(8,128)(2,1)}, u32[]{:S(2)}) copy-start(bf16[384,96]{0,1:T(8,128)(2,1)} %param.22) | copy-start | bytes 221188
  29.7 27.3 %copy-start.12 = (f32[96]{0:T(128)S(1)}, f32[96]{0:T(128)}, u32[]{:S(2)}) copy-start(f32[96]{0:T(128)} %param.23) | copy-start | bytes 1156
  29.7 27.6 %copy-start.9 = (s32[1024]{0:T(1024)S(1)}, s32[1024]{0:T(1024)}, u32[]{:S(2)}) copy-start(s32[1024]{0:T(1024)} %param.16) | copy-start | bytes 12292
  29.8 49.7 %copy-start.3 = (bf16[384,96]{0,1:T(8,128)(2,1)S(1)}, bf16[384,96]{0,1:T(8,128)(2,1)}, u32[]{:S(2)}) copy-start(bf16[384,96]{0,1:T(8,128)(2,1)} %param.25) | copy-start | bytes 221188
  29.8 49.7 %copy-start.4 = (bf16[384,96]{0,1:T(8,128)(2,1)S(1)}, bf16[384,96]{0,1:T(8,128)(2,1)}, u32[]{:S(2)}) copy-start(bf16[384,96]{0,1:T(8,128)(2,1)} %param.24) | copy-start | bytes 221188
  30.9 50.2 %copy-start.2 = (bf16[384,96]{0,1:T(8,128)(2,1)S(1)}, bf16[384,96]{0,1:T(8,128)(2,1)}, u32[]{:S(2)}) copy-start(bf16[384,96]{0,1:T(8,128)(2,1)} %param.26) | copy-start | bytes 221188
  31.9 13.8 %all-to-all-start.1 = ((bf16[16,64,256]{2,1,0:T(8,128)(2,1)}), bf16[16,64,256]{2,1,0:T(8,128)(2,1)S(1)}, u32[]{:S(2)}, u32[]{:S(2)}) async-start(bf16[16,64,256]{2,1,0:T(8,128)(2,1)} %bitcast.28), calls=%async_computation.1 | async-start | bytes 1048576 | tf_op jit(solution)/shard_map/all_to_all | solution.py:76
  46.6 32.9 %all-to-all-start = ((bf16[16,64,384]{2,1,0:T(8,128)(2,1)}), bf16[16,64,384]{2,1,0:T(8,128)(2,1)S(1)}, u32[]{:S(2)}, u32[]{:S(2)}) async-start(bf16[16,64,384]{2,1,0:T(8,128)(2,1)} %stack.2), calls=%async_computation | async-start | bytes 1572864 | tf_op jit(solution)/shard_map/all_to_all | solution.py:83
  56.9 43.4 %reduce-scatter.4.cloned.1.call-start = ((), (), s32[]{:S(2)}) async-start(), calls=%async_computation.3 | async-start | bytes 245760
Sparse Core Ops, SparseCore 0:
  82.4 17.8 reduce-scatter.3
